TPU v7x, 32 devices: a whole 2x2x4 slice. The times are simulated.
32 devices in a mesh: seq: 8 (over z, x), head: 4 (over y, core).
Axes of the slice: x: 2, y: 2, z: 4, core: 2. Of those that a mesh axis runs over, the one named last changes fastest.
Arguments:
- queries: bfloat16 [2048, 4096], P('seq', 'head'), may hold values from -1.796875 to 1.796875
- key_vectors: bfloat16 [2048, 4096], P('seq', 'head'), may hold values from -1.796875 to 1.796875
- values: bfloat16 [2048, 4096], P('seq', 'head'), may hold values from -96 to 96
- decay_log: float32 [32, 2048], P('head', 'seq'), may hold values from -2 to 0
- doc_starts: int32 [8, 4], P('seq'), may hold values from 0 to 256, as said below
- gate_logits: bfloat16 [2048, 4096], P('seq', 'head'), may hold values from -6 to 6
- norm_gain: float32 [4096], P('head'), may hold values from 0.1 to 1.9
- grad_out: bfloat16 [2048, 4096], P('seq', 'head'), may hold values from -6 to 6
Outputs:
- grad_query: bfloat16 [2048, 4096], P('seq', 'head')
- grad_key: bfloat16 [2048, 4096], P('seq', 'head')
- grad_value: bfloat16 [2048, 4096], P('seq', 'head')
- grad_gate: bfloat16 [2048, 4096], P('seq', 'head')
Inputs may be any that keep to these rules, and one draw needn't show every extreme that they name: `doc_starts`: each row lists in rising order the offsets within its shard of 256 tokens at which documents start, then 256 in unused places; some shard has 4 starts, the first at 0, and some shard has none.
All inputs are finite; a program needn't handle non-finite values.
Results may differ from a plain program's by a relative error of at most 0.0057.
Values sent between devices are 32-bit elements; how exact they have to be, the bound alone decides.
A program may use at most 128 MiB of HBM per device.

v0:
```python
import jax
import jax.numpy as jnp
from jax import lax
from jax.sharding import PartitionSpec as P

HEAD_DIM = 128
BLOCK = 256


highest = lax.Precision.HIGHEST
epsilon = 1e-06


def prefix(part, axis, combine, identity, reverse):
    count = lax.axis_size(axis)
    place = lax.axis_index(axis)
    ahead = count - 1 - place if reverse else place
    gathered = jax.tree.map(lambda a: lax.all_gather(a, axis), part)
    state = jax.tree.map(lambda a, e: jnp.zeros_like(a) + jnp.asarray(e, a.dtype), part, identity)

    def one(turn, state):
        source = count - 1 - turn if reverse else turn
        return combine(
            state, jax.tree.map(lambda a: lax.dynamic_index_in_dim(a, source, 0, False), gathered)
        )

    return lax.fori_loop(0, ahead, one, state)


def block_factors(decay_block, start_block):
    counted = jnp.cumsum(start_block, axis=-1)
    summed = jnp.cumsum(decay_block, axis=-1)
    length = start_block.shape[-1]
    element_slots_along_text = jnp.arange(length)
    causal = element_slots_along_text[:, None] >= element_slots_along_text[None, :]
    keeper = jnp.logical_and(causal[None], counted[:, :, None] == counted[:, None, :])[:, None]
    spread = summed[:, :, :, None] - summed[:, :, None, :]
    multiplier = jnp.where(keeper, jnp.exp(jnp.where(keeper, spread, 0.0)), 0.0)
    inward = jnp.where((counted == 0)[:, None, :], jnp.exp(summed), 0.0)
    latest = counted[:, -1:]
    outward = jnp.where((counted == latest)[:, None, :], jnp.exp(summed[:, :, -1:] - summed), 0.0)
    through = jnp.where(latest == 0, jnp.exp(summed[:, :, -1]), 0.0)
    return (multiplier, inward, outward, through)


def link_states(earlier, later):
    return (earlier[0] * later[0], later[0][:, None, None] * earlier[1] + later[1])


def local_chain(through, sums_here, backward):

    def advance(carried, pieces):
        memory, factor = carried
        rate_here, addition = pieces
        return (
            (rate_here[:, None, None] * memory + addition, factor * rate_here),
            (memory, factor),
        )

    initial = (jnp.zeros_like(sums_here[0]), jnp.ones_like(through[0]))
    closing, before = lax.scan(advance, initial, (through, sums_here), reverse=backward)
    return (closing, before)


def local(queries, key_vectors, values, decay_log, doc_starts, gate_logits, norm_gain, grad_out):
    tok_count = queries.shape[0]
    heads_here = queries.shape[1] // HEAD_DIM
    count_blocks = tok_count // BLOCK
    features = queries.shape[1] * lax.axis_size("head")
    element_slots_along_text = jnp.arange(tok_count, dtype=jnp.int32)
    start_marks = jnp.any(
        doc_starts[0][:, None] == element_slots_along_text[None, :], axis=0
    ).astype(jnp.int32)
    start_marks = start_marks.reshape(count_blocks, BLOCK)
    decays = decay_log.reshape(heads_here, count_blocks, BLOCK).transpose(1, 0, 2)

    def shaped(array):
        return array.reshape(count_blocks, BLOCK, heads_here, HEAD_DIM)

    query_blocks = shaped(queries)
    key_blocks = shaped(key_vectors)
    value_blocks = shaped(values)
    multiplier, inward, outward, through = block_factors(decays, start_marks)
    inward_rows = inward.transpose(0, 2, 1)[..., None]
    outward_rows = outward.transpose(0, 2, 1)[..., None]
    scores = jnp.einsum(
        "nthd,nshd->nhts", query_blocks, key_blocks, preferred_element_type=jnp.float32
    )
    mixing = (multiplier * scores).astype(jnp.bfloat16)
    within = jnp.einsum("nhts,nshd->nthd", mixing, value_blocks, preferred_element_type=jnp.float32)
    key_scaled = (key_blocks.astype(jnp.float32) * outward_rows).astype(jnp.bfloat16)
    sums_here = jnp.einsum(
        "nshd,nshe->nhde", key_scaled, value_blocks, preferred_element_type=jnp.float32
    )
    (summary, through_dev), (starts_local, factors_local) = local_chain(through, sums_here, False)
    _, incoming = prefix(
        (through_dev, summary),
        "seq",
        link_states,
        (jnp.ones_like(through_dev), jnp.zeros_like(summary)),
        False,
    )
    incoming_state = factors_local[:, :, None, None] * incoming[None] + starts_local
    carried = (
        jnp.einsum(
            "nthd,nhde->nthe",
            query_blocks,
            incoming_state,
            precision=highest,
            preferred_element_type=jnp.float32,
        )
        * inward_rows
    )
    attended = (within + carried).reshape(tok_count, queries.shape[1])
    opening = jax.nn.sigmoid(gate_logits.astype(jnp.float32))
    upstream = grad_out.astype(jnp.float32)
    dnormed = upstream * norm_gain[None, :] * opening
    squares = jnp.sum(attended * attended, axis=1)
    totals = lax.psum(squares, "head")
    spread_rms = jnp.sqrt(totals / features + epsilon)
    normed = attended / spread_rms[:, None]
    projection = lax.psum(jnp.sum(dnormed * normed, axis=1), "head") / features
    grad_gate = (upstream * norm_gain[None, :] * normed * opening * (1.0 - opening)).astype(
        jnp.bfloat16
    )
    grad_attn = ((dnormed - normed * projection[:, None]) / spread_rms[:, None]).astype(
        jnp.bfloat16
    )
    grad_blocks = shaped(grad_attn)
    query_scaled = (query_blocks.astype(jnp.float32) * inward_rows).astype(jnp.bfloat16)
    back_sums = jnp.einsum(
        "nthd,nthe->nhde", query_scaled, grad_blocks, preferred_element_type=jnp.float32
    )
    (back_summary, _), (reverse_inner_product, back_factors) = local_chain(through, back_sums, True)
    _, arriving = prefix(
        (through_dev, back_summary),
        "seq",
        link_states,
        (jnp.ones_like(through_dev), jnp.zeros_like(back_summary)),
        True,
    )
    leaving = back_factors[:, :, None, None] * arriving[None] + reverse_inner_product
    scores_gradient = jnp.einsum(
        "nthe,nshe->nhts", grad_blocks, value_blocks, preferred_element_type=jnp.float32
    )
    grad_mixing = (multiplier * scores_gradient).astype(jnp.bfloat16)
    grad_query = jnp.einsum(
        "nhts,nshd->nthd", grad_mixing, key_blocks, preferred_element_type=jnp.float32
    )
    grad_query = (
        grad_query
        + jnp.einsum(
            "nthe,nhde->nthd",
            grad_blocks,
            incoming_state,
            precision=highest,
            preferred_element_type=jnp.float32,
        )
        * inward_rows
    )
    grad_key = jnp.einsum(
        "nhts,nthd->nshd", grad_mixing, query_blocks, preferred_element_type=jnp.float32
    )
    grad_key = (
        grad_key
        + jnp.einsum(
            "nshe,nhde->nshd",
            value_blocks,
            leaving,
            precision=highest,
            preferred_element_type=jnp.float32,
        )
        * outward_rows
    )
    grad_value = jnp.einsum(
        "nhts,nthe->nshe", mixing, grad_blocks, preferred_element_type=jnp.float32
    )
    grad_value = (
        grad_value
        + jnp.einsum(
            "nshd,nhde->nshe",
            key_blocks,
            leaving,
            precision=highest,
            preferred_element_type=jnp.float32,
        )
        * outward_rows
    )
    width = queries.shape[1]
    return (
        grad_query.reshape(tok_count, width).astype(jnp.bfloat16),
        grad_key.reshape(tok_count, width).astype(jnp.bfloat16),
        grad_value.reshape(tok_count, width).astype(jnp.bfloat16),
        grad_gate,
    )


def solution(mesh):
    placed = (
        P("seq", "head"),
        P("seq", "head"),
        P("seq", "head"),
        P("head", "seq"),
        P("seq", None),
        P("seq", "head"),
        P("head"),
        P("seq", "head"),
    )
    return jax.shard_map(
        local,
        mesh=mesh,
        in_specs=placed,
        out_specs=(P("seq", "head"), P("seq", "head"), P("seq", "head"), P("seq", "head")),
        check_vma=False,
    )
```

profile of v0, /device:TPU:0, one launch (start us, length us, event | category | flops | bytes accessed | tf_op | source)
XLA Modules:
  0.0 214.6 jit_solution(485621590473710357)
XLA Ops:
  7.2 1.3 reduce-window.16
  11.5 1.2 copy.135
  16.2 22.2 %all-gather = f32[8,8,1]{1,2,0:T(1,128)S(1)} all-gather(f32[1,8,1]{1,2,0:T(1,128)S(1)} %copy.109), channel_id=2, replica_groups=mesh['seq'=8,'head'=4] {'seq'}, dimensions={0}, use_global_device_ids=true | all-gather | bytes 288 | tf_op jit(solution)/shard_map/all_gather | solution.py:18
  40.9 51.2 %all-gather.6.cloned.1.call-done = f32[64,128,128]{2,1,0:T(8,128)} async-done(((f32[8,128,128]{2,1,0:T(8,128)}), f32[64,128,128]{2,1,0:T(8,128)}) %all-gather.6.cloned.1.call-update) | async-done | bytes 4194320 | tf_op jit(solution)/shard_map/all_gather | solution.py:18
  92.1 1.7 multiply_reduce_fusion.1
  93.8 1.6 copy.114
  95.4 5.7 %psum.14 = f32[256]{0:T(256)S(1)} all-reduce(f32[256]{0:T(256)S(1)} %get-tuple-element.224), channel_id=1, replica_groups=mesh['seq'=8,'head'=4] {'head'}, use_global_device_ids=true, to_apply=%region_8.9 | all-reduce | flops 256 | bytes 2048 | tf_op jit(solution)/shard_map/psum | solution.py:119
  101.1 1.7 multiply_reduce_fusion
  102.7 6.6 %psum.15 = f32[256]{0:T(256)S(1)} all-reduce(f32[256]{0:T(256)S(1)} %multiply_reduce_fusion), channel_id=1, replica_groups=mesh['seq'=8,'head'=4] {'head'}, use_global_device_ids=true, to_apply=%region_10.11 | all-reduce | flops 256 | bytes 2048 | tf_op jit(solution)/shard_map/psum | solution.py:122
  109.3 2.8 %multiply_convert_fusion.2 = (bf16[256,1024]{1,0:T(8,128)(2,1)}, bf16[256,1024]{1,0:T(8,128)(2,1)}) fusion(bf16[256,1024]{1,0:T(8,128)(2,1)} %param.19, f32[1024]{0:T(1024)S(1)} %copy-done.8, bf16[256,1024]{1,0:T(8,128)(2,1)} %param.17, f32[256,1024]{1,0:T(8,128)S(1)} %copy.114, f32[256]{0:T(256)S(1)} %add_sqrt_fusion, f32[256]{0:T(256)S(1)} %broadcast_multiply_fusion), kind=kLoop, calls=%fused_computation.28 | loop fusion | flops 4456448 | bytes 3151872 | tf_op jit(solution)/shard_map/convert_element_type | solution.py:123
  112.1 1.2 copy.132
  115.7 1.4 fusion.10
  117.1 2.1 copy.126
  119.3 2.5 %convolution_bitcast_fusion.4 = f32[1,256,8,128]{1,3,2,0:T(8,128)} fusion(bf16[256,8,128]{0,2,1:T(8,128)(2,1)S(1)} %bitcast.182, bf16[8,256,256]{2,1,0:T(8,128)(2,1)} %copy-done.4), kind=kOutput, calls=%fused_computation.11 | convolution fusion | flops 134217728 | bytes 2621440 | tf_op jit(solution)/shard_map/nhts,nthd->nshd/dot_general | solution.py:161
  121.8 1.3 convolution_bitcast_fusion.5
  123.1 71.4 %all-gather.8.cloned.1.call-done = f32[64,128,128]{2,1,0:T(8,128)} async-done(((f32[8,128,128]{2,1,0:T(8,128)}), f32[64,128,128]{2,1,0:T(8,128)}) %all-gather.8.cloned.1.call-update) | async-done | bytes 4194320 | tf_op jit(solution)/shard_map/all_gather | solution.py:18
  194.5 8.6 %while.17 = (s32[]{:T(128)}, f32[8,128,128]{2,1,0:T(8,128)S(1)}, s32[]{:T(128)}, f32[8,8]{1,0:T(8,128)S(1)}, f32[8,8,128,128]{3,2,1,0:T(8,128)}, /*index=5*/s32[]{:T(128)}, s32[]{:T(128)}, s32[]{:T(128)}, s32[]{:T(128)}) while((s32[]{:T(128)}, f32[8,128,128]{2,1,0:T(8,128)S(1)}, s32[]{:T(128)}, f32[8,8]{1,0:T(8,128)S(1)}, ...), condition=%wide.region_12.13_spmd, body=%wide.region_11.12_spmd.sunk | while | flops 262150 | bytes 1573115 | solution.py:27
  194.6 1.2 bitcast_add_fusion.10
  195.8 1.2 bitcast_add_fusion.10
  197.0 1.2 bitcast_add_fusion.10
  198.3 1.2 bitcast_add_fusion.10
  199.5 1.2 bitcast_add_fusion.10
  200.7 1.2 bitcast_add_fusion.10
  203.2 1.9 fusion.9
  (67 shorter events, 13.9 us)
Async XLA Ops:
  7.2 7.5 %copy-start = (bf16[256,1024]{1,0:T(8,128)(2,1)S(1)}, bf16[256,1024]{1,0:T(8,128)(2,1)}, u32[]{:S(2)}) copy-start(bf16[256,1024]{1,0:T(8,128)(2,1)} %param.14) | copy-start | bytes 1572868
  7.2 84.9 %all-gather.6.cloned.1.call-start = ((), (), s32[]{:S(2)}) async-start(), calls=%async_computation | async-start | bytes 4718592 | tf_op jit(solution)/shard_map/all_gather | solution.py:18
  11.5 4.4 %copy-start.7 = (bf16[256,1024]{1,0:T(8,128)(2,1)S(1)}, bf16[256,1024]{1,0:T(8,128)(2,1)}, u32[]{:S(2)}) copy-start(bf16[256,1024]{1,0:T(8,128)(2,1)} %param.12) | copy-start | bytes 1572868
  12.7 25.9 %copy-start.5 = (bf16[256,1024]{1,0:T(8,128)(2,1)S(1)}, bf16[256,1024]{1,0:T(8,128)(2,1)}, u32[]{:S(2)}) copy-start(bf16[256,1024]{1,0:T(8,128)(2,1)} %param.13) | copy-start | bytes 1572868
  15.8 178.7 %all-gather.8.cloned.1.call-start = ((), (), s32[]{:S(2)}) async-start(), calls=%async_computation.1 | async-start | bytes 4718592 | tf_op jit(solution)/shard_map/all_gather | solution.py:18
  39.4 1.0 copy-start.1
  92.1 8.9 %copy-start.8 = (f32[1024]{0:T(1024)S(1)}, f32[1024]{0:T(1024)}, u32[]{:S(2)}) copy-start(f32[1024]{0:T(1024)} %param.18) | copy-start | bytes 12292
  115.3 1.9 copy-start.4
  117.1 4.6 %copy-start.2 = (bf16[8,256,256]{2,1,0:T(8,128)(2,1)S(1)}, bf16[8,256,256]{2,1,0:T(8,128)(2,1)}, u32[]{:S(2)}) copy-start(bf16[8,256,256]{2,1,0:T(8,128)(2,1)} %copy-done.1) | copy-start | bytes 3145732
  203.2 3.0 %copy-start.3 = (f32[1,256,8,128]{1,3,2,0:T(8,128)S(1)}, f32[1,256,8,128]{1,3,2,0:T(8,128)}, u32[]{:S(2)}) copy-start(f32[1,256,8,128]{1,3,2,0:T(8,128)} %convolution_bitcast_fusion.5) | copy-start | bytes 3145732
  203.2 3.0 %copy-start.6 = (bf16[256,1024]{1,0:T(8,128)(2,1)S(1)}, bf16[256,1024]{1,0:T(8,128)(2,1)}, u32[]{:S(2)}) copy-start(bf16[256,1024]{1,0:T(8,128)(2,1)} %param.13) | copy-start | bytes 1572868
Sparse Core Ops, SparseCore 0:
  15.9 76.0 all-gather.5
  114.6 79.8 all-gather.7
where the time goes:
time: 215 us
  waiting for transfers between devices  123 us (57%)
  blocking collectives  34.5 us (16%)
  other arithmetic  16 us (7%)
  between operations  15.6 us (7%)
  matrix products  14.2 us (7%)
  local copies, waits for them, and re-layouts  11.5 us (5%)
    all_gather x2, waiting for transfers between devices, prefix(): gathered = jax.tree.map(lambda a: lax.all_gather(a, axis), part)  123 us
    all_gather x1, blocking collectives, prefix(): gathered = jax.tree.map(lambda a: lax.all_gather(a, axis), part)  22.2 us
    add x7, other arithmetic, link_states(): later[0][:, None, None] * earlier[1] + later[1]  8.33 us
    psum x1, blocking collectives, local(): projection = lax.psum(jnp.sum(dnormed * normed, axis=1), 'head') / features  6.6 us
    unnamed x22, local copies, waits for them, and re-layouts  6.38 us
    psum x1, blocking collectives, local(): totals = lax.psum(squares, 'head')  5.67 us
  transfers between devices with their start and end apart: 2, of which 2 were waited for; matrix products, arithmetic and copies ran while one was open for 5% of the time, Pallas kernels for 0%

commit v1 on v0

v1 whole, which is shorter than its diff:
```python
import functools

import jax
import jax.numpy as jnp
from jax import lax
from jax.experimental import pallas as pl
from jax.experimental.pallas import tpu as pltpu
from jax.sharding import PartitionSpec as P

HEAD_DIM = 128
EPSILON = 1e-06
MESH = pl.DeviceIdType.MESH
F32 = jnp.float32
BF16 = jnp.bfloat16
HIGHEST = lax.Precision.HIGHEST


def mm(a, b, ca, cb, precision=None):
    return lax.dot_general(
        a, b, (((ca,), (cb,)), ((), ())), precision=precision, preferred_element_type=F32
    )


def kernel(
    n_seq,
    n_head,
    q_ref,
    k_ref,
    v_ref,
    decay_ref,
    starts_ref,
    gate_ref,
    gain_ref,
    gout_ref,
    dq_ref,
    dk_ref,
    dv_ref,
    dgate_ref,
    mine_ref,
    theirs_ref,
    onward_ref,
    inbound_ref,
    through_ref,
    enter_ref,
    weight_ref,
    mixing_ref,
    attended_ref,
    dnormed_ref,
    dgate_part_ref,
    qscaled_ref,
    dk_part_ref,
    dv_part_ref,
    bias_ref,
    sums_ref,
    state_send,
    state_recv,
    chain_send,
    chain_recv,
    through_sem,
    sums_send,
    sums_recv,
):
    tokens, width = q_ref.shape
    heads = width // HEAD_DIM
    features = width * n_head
    seq = lax.axis_index("seq")
    head = lax.axis_index("head")
    side = lax.rem(seq, 2)
    link = seq // 2
    links = n_seq // 2
    first = side == 0
    partner = seq + 1 - 2 * side

    def cols(h):
        return slice(h * HEAD_DIM, (h + 1) * HEAD_DIM)

    barrier = pltpu.get_barrier_semaphore()

    def greet(s, h):
        pl.semaphore_signal(barrier, inc=1, device_id={"seq": s, "head": h}, device_id_type=MESH)

    greet(partner, head)
    for d in range(1, n_head):
        greet(seq, lax.rem(head + d, n_head))

    @pl.when(link > 0)
    def _():
        greet(seq - 2, head)

    @pl.when(link < links - 1)
    def _():
        greet(seq + 2, head)

    row_ids = lax.broadcasted_iota(jnp.int32, (tokens, tokens), 0)
    col_ids = lax.broadcasted_iota(jnp.int32, (tokens, tokens), 1)
    causal = row_ids >= col_ids
    lower = causal.astype(F32)
    decay = decay_ref[...]
    sum_row = mm(decay, lower, 1, 1, HIGHEST)
    sum_col = mm(lower, decay, 1, 1, HIGHEST)
    ids_col = lax.broadcasted_iota(jnp.int32, (tokens, 1), 0)
    ids_row = lax.broadcasted_iota(jnp.int32, (1, tokens), 1)
    count_col = jnp.zeros((tokens, 1), jnp.int32)
    count_row = jnp.zeros((1, tokens), jnp.int32)
    latest = jnp.int32(0)
    for j in range(starts_ref.shape[1]):
        start = starts_ref[0, j]
        count_col += (ids_col >= start).astype(jnp.int32)
        count_row += (ids_row >= start).astype(jnp.int32)
        latest += (start < tokens).astype(jnp.int32)
    inward = jnp.where(count_col == 0, jnp.exp(sum_col), 0.0)
    outward = jnp.where(
        count_col == latest, jnp.exp(sum_col[tokens - 1 : tokens, :] - sum_col), 0.0
    )
    through = jnp.where(latest == 0, jnp.exp(sum_row[:, tokens - 1 : tokens]), 0.0)
    through_ref[0] = jnp.broadcast_to(through, (heads, HEAD_DIM))
    keep = jnp.logical_and(causal, count_col == count_row)
    bias_ref[...] = jnp.where(keep, 0.0, -1e30)

    def remote(src, dst, send, recv, s, h):
        return pltpu.make_async_remote_copy(
            src_ref=src,
            dst_ref=dst,
            send_sem=send,
            recv_sem=recv,
            device_id={"seq": s, "head": h},
            device_id_type=MESH,
        )

    through_copy = remote(
        through_ref.at[0], through_ref.at[1], through_sem.at[0], through_sem.at[1], partner, head
    )

    def exchange(way, h):
        return remote(
            mine_ref.at[way, h],
            theirs_ref.at[way, h],
            state_send.at[way, h],
            state_recv.at[way, h],
            partner,
            head,
        )

    def chain(way, h):
        target = seq + 2 if way == 0 else seq - 2
        return remote(
            onward_ref.at[way, h],
            inbound_ref.at[way, h],
            chain_send.at[way, h],
            chain_recv.at[way, h],
            target,
            head,
        )

    def has_next(way):
        return link < links - 1 if way == 0 else link > 0

    def has_previous(way):
        return link > 0 if way == 0 else link < links - 1

    def pass_on(way, h):
        leads = first if way == 0 else jnp.logical_not(first)
        exchange(way, h).wait_recv()
        mine = mine_ref[way, h]
        theirs = theirs_ref[way, h]
        t_mine = through_ref[0, h : h + 1, :]
        t_theirs = through_ref[1, h : h + 1, :]
        pair = jnp.where(leads, t_theirs, 1.0) * mine + jnp.where(leads, 1.0, t_mine) * theirs

        @pl.when(has_previous(way))
        def _():
            chain(way, h).wait_recv()

        arrived = inbound_ref[way, h]

        @pl.when(has_next(way))
        def _():
            onward_ref[way, h] = t_mine * t_theirs * arrived + pair
            chain(way, h).start()

        return jnp.where(leads, 1.0, t_theirs) * arrived + jnp.where(leads, 0.0, 1.0) * theirs

    for way in range(2):

        @pl.when(jnp.logical_not(has_previous(way)))
        def _():
            inbound_ref[way] = jnp.zeros(inbound_ref.shape[1:], F32)

    pl.semaphore_wait(
        barrier,
        n_head + (link > 0).astype(jnp.int32) + (link < links - 1).astype(jnp.int32),
    )
    through_copy.start()
    for h in range(heads):
        scaled = (k_ref[:, cols(h)].astype(F32) * outward[:, h : h + 1]).astype(BF16)
        mine_ref[0, h] = mm(scaled, v_ref[:, cols(h)], 0, 0)
        exchange(0, h).start()

    def within(h):
        q = q_ref[:, cols(h)]
        weight = jnp.exp(sum_col[:, h : h + 1] - sum_row[h : h + 1, :] + bias_ref[...])
        weight_ref[h] = weight
        mixing = (weight * mm(q, k_ref[:, cols(h)], 1, 1)).astype(BF16)
        mixing_ref[h] = mixing
        attended_ref[:, cols(h)] = mm(mixing, v_ref[:, cols(h)], 1, 0)
        qscaled_ref[:, cols(h)] = (q.astype(F32) * inward[:, h : h + 1]).astype(BF16)
        opening = jax.nn.sigmoid(gate_ref[:, cols(h)].astype(F32))
        dnormed = gout_ref[:, cols(h)].astype(F32) * gain_ref[:, cols(h)] * opening
        dnormed_ref[:, cols(h)] = dnormed
        dgate_part_ref[:, cols(h)] = dnormed * (1.0 - opening)

    squares = jnp.zeros((tokens, HEAD_DIM), F32)
    products = jnp.zeros((tokens, HEAD_DIM), F32)
    ahead = 2
    for h in range(min(ahead, heads)):
        within(h)
    through_copy.wait_recv()
    for h in range(heads):
        state = pass_on(0, h).astype(BF16)
        enter_ref[h] = state
        attended = attended_ref[:, cols(h)] + inward[:, h : h + 1] * mm(
            q_ref[:, cols(h)], state, 1, 0
        )
        attended_ref[:, cols(h)] = attended
        squares += attended * attended
        products += dnormed_ref[:, cols(h)] * attended
        if h + ahead < heads:
            within(h + ahead)

    ones = jnp.ones((8, HEAD_DIM), F32)
    square_rows = mm(ones, squares, 1, 1, HIGHEST)
    product_rows = mm(ones, products, 1, 1, HIGHEST)
    sum_ids = lax.broadcasted_iota(jnp.int32, (8, tokens), 0)
    sums_ref[0] = jnp.where(sum_ids == 0, square_rows, product_rows)
    sum_copies = [
        remote(
            sums_ref.at[0],
            sums_ref.at[d],
            sums_send.at[d - 1],
            sums_recv.at[d - 1],
            seq,
            lax.rem(head + d, n_head),
        )
        for d in range(1, n_head)
    ]
    for copy in sum_copies:
        copy.start()
    for copy in sum_copies:
        copy.wait_recv()
    totals = sums_ref[0]
    for d in range(1, n_head):
        totals += sums_ref[d]
    totals = totals / features
    inverse = lax.rsqrt(totals[0:1] + EPSILON)
    pull = totals[1:2] * inverse * inverse * inverse
    scalars = jnp.where(sum_ids == 0, inverse, pull)
    unit = (
        lax.broadcasted_iota(jnp.int32, (8, 8), 0) == lax.broadcasted_iota(jnp.int32, (8, 8), 1)
    ).astype(F32)
    scalars = mm(scalars, unit, 0, 0, HIGHEST)
    inverse = scalars[:, 0:1]
    pull = scalars[:, 1:2]

    grads = []
    for h in range(heads):
        grad = (dnormed_ref[:, cols(h)] * inverse - attended_ref[:, cols(h)] * pull).astype(BF16)
        grads.append(grad)
        mine_ref[1, h] = mm(qscaled_ref[:, cols(h)], grad, 0, 0)
        exchange(1, h).start()

    def inside(h):
        q = q_ref[:, cols(h)]
        k = k_ref[:, cols(h)]
        v = v_ref[:, cols(h)]
        grad = grads[h]
        grad_mixing = (weight_ref[h] * mm(grad, v, 1, 1)).astype(BF16)
        dq = mm(grad_mixing, k, 1, 0) + inward[:, h : h + 1] * mm(grad, enter_ref[h], 1, 1)
        dq_ref[:, cols(h)] = dq.astype(BF16)
        dk_part_ref[:, cols(h)] = mm(grad_mixing, q, 0, 0)
        dv_part_ref[:, cols(h)] = mm(mixing_ref[h], grad, 0, 0)
        dgate_ref[:, cols(h)] = (
            dgate_part_ref[:, cols(h)] * attended_ref[:, cols(h)] * inverse
        ).astype(BF16)

    for h in range(min(ahead, heads)):
        inside(h)
    for h in range(heads):
        state = pass_on(1, h).astype(BF16)
        scale = outward[:, h : h + 1]
        dk = dk_part_ref[:, cols(h)] + scale * mm(v_ref[:, cols(h)], state, 1, 1)
        dv = dv_part_ref[:, cols(h)] + scale * mm(k_ref[:, cols(h)], state, 1, 0)
        dk_ref[:, cols(h)] = dk.astype(BF16)
        dv_ref[:, cols(h)] = dv.astype(BF16)
        if h + ahead < heads:
            inside(h + ahead)

    through_copy.wait_send()
    for copy in sum_copies:
        copy.wait_send()
    for way in range(2):
        for h in range(heads):
            exchange(way, h).wait_send()

        @pl.when(has_next(way))
        def _():
            for h in range(heads):
                chain(way, h).wait_send()


def local(queries, key_vectors, values, decay_log, doc_starts, gate_logits, norm_gain, grad_out):
    n_seq = lax.axis_size("seq")
    n_head = lax.axis_size("head")
    tokens, width = queries.shape
    heads = width // HEAD_DIM
    vmem = pl.BlockSpec(memory_space=pltpu.VMEM)
    smem = pl.BlockSpec(memory_space=pltpu.SMEM)
    states = (2, heads, HEAD_DIM, HEAD_DIM)
    out = jax.ShapeDtypeStruct((tokens, width), BF16)
    return pl.pallas_call(
        functools.partial(kernel, n_seq, n_head),
        out_shape=(out, out, out, out),
        in_specs=[vmem, vmem, vmem, vmem, smem, vmem, vmem, vmem],
        out_specs=(vmem, vmem, vmem, vmem),
        scratch_shapes=[
            pltpu.VMEM(states, F32),
            pltpu.VMEM(states, F32),
            pltpu.VMEM(states, F32),
            pltpu.VMEM(states, F32),
            pltpu.VMEM((2, heads, HEAD_DIM), F32),
            pltpu.VMEM((heads, HEAD_DIM, HEAD_DIM), BF16),
            pltpu.VMEM((heads, tokens, tokens), F32),
            pltpu.VMEM((heads, tokens, tokens), BF16),
            pltpu.VMEM((tokens, width), F32),
            pltpu.VMEM((tokens, width), F32),
            pltpu.VMEM((tokens, width), F32),
            pltpu.VMEM((tokens, width), BF16),
            pltpu.VMEM((tokens, width), F32),
            pltpu.VMEM((tokens, width), F32),
            pltpu.VMEM((tokens, tokens), F32),
            pltpu.VMEM((n_head, 8, tokens), F32),
            pltpu.SemaphoreType.DMA((2, heads)),
            pltpu.SemaphoreType.DMA((2, heads)),
            pltpu.SemaphoreType.DMA((2, heads)),
            pltpu.SemaphoreType.DMA((2, heads)),
            pltpu.SemaphoreType.DMA((2,)),
            pltpu.SemaphoreType.DMA((max(n_head - 1, 1),)),
            pltpu.SemaphoreType.DMA((max(n_head - 1, 1),)),
        ],
        compiler_params=pltpu.CompilerParams(
            collective_id=0, has_side_effects=True, vmem_limit_bytes=48 * 1024 * 1024
        ),
        name="attention_both_ways",
    )(
        queries,
        key_vectors,
        values,
        decay_log,
        doc_starts,
        gate_logits,
        norm_gain.reshape(1, width),
        grad_out,
    )


def solution(mesh):
    placed = (
        P("seq", "head"),
        P("seq", "head"),
        P("seq", "head"),
        P("head", "seq"),
        P("seq", None),
        P("seq", "head"),
        P("head"),
        P("seq", "head"),
    )
    return jax.shard_map(
        local,
        mesh=mesh,
        in_specs=placed,
        out_specs=(P("seq", "head"), P("seq", "head"), P("seq", "head"), P("seq", "head")),
        check_vma=False,
    )
```

time: 215 us -> 67.1 us (0.31)
  waiting for transfers between devices: 123 us -> 0 us
  Pallas kernels: 0 us -> 55.6 us
  blocking collectives: 34.5 us -> 0 us
  other arithmetic: 16 us -> 0 us
  between operations: 15.6 us -> 0.66 us
  matrix products: 14.2 us -> 0 us
    all_gather x2 -> x0, waiting for transfers between devices: 123 us -> none  [prefix(): gathered = jax.tree.map(lambda a: lax.all_gather(a, axis), part)]
    pallas_call x0 -> x1, Pallas kernels: none -> 55.6 us  [local(): pl.pallas_call(functools.partial(kernel, n_seq, n_head), out_shape=(out,...]
    all_gather x1 -> x0, blocking collectives: 22.2 us -> none  [prefix(): gathered = jax.tree.map(lambda a: lax.all_gather(a, axis), part)]
    dot_general x12 -> x0, matrix products: 14.2 us -> none  [the longest x1 2.51 us: local(): jnp.einsum('nhts,nthd->nshd', grad_mixing, query_blocks, preferred_elemen...]
    psum x2 -> x0, blocking collectives: 12.3 us -> none  [the longest x1 6.6 us: local(): projection = lax.psum(jnp.sum(dnormed * normed, axis=1), 'head') / features]
    add x7 -> x0, other arithmetic: 8.33 us -> none  [link_states(): later[0][:, None, None] * earlier[1] + later[1]]
    unnamed x22 -> x20, local copies, waits for them, and re-layouts: 6.38 us -> 10.4 us
    convert_element_type x2 -> x0, other arithmetic: 2.77 us -> none  [the longest x1 2.77 us: local(): (upstream * norm_gain[None, :] * normed * opening * (1.0 - opening)).asty...]
  transfers between devices with their start and end apart: 2 -> 0, of which waited for: 2 -> 0; matrix products, arithmetic and copies ran while one was open for 5% -> 0% of each run, Pallas kernels for 0% -> 0%
where the time goes in v1:
time: 67.1 us; the launch traced here: 66.6 us
  Pallas kernels  55.6 us (83%)
  local copies, waits for them, and re-layouts  10.4 us (15%)
    pallas_call x1, Pallas kernels, local(): pl.pallas_call(functools.partial(kernel, n_seq, n_head), out_shape=(out,...  55.6 us
    unnamed x20, local copies, waits for them, and re-layouts  10.4 us

profile of v1, /device:TPU:0, one launch (start us, length us, event | category | flops | bytes accessed | tf_op | source)
XLA Modules:
  0.0 66.6 jit_solution(13612424803908122067)
XLA Ops:
  0.6 0.0 copy-start.7
  0.6 0.6 copy-done.7
  1.3 0.0 copy-start
  1.3 1.0 %copy-done = bf16[256,1024]{1,0:T(8,128)(2,1)S(1)} copy-done((bf16[256,1024]{1,0:T(8,128)(2,1)S(1)}, bf16[256,1024]{1,0:T(8,128)(2,1)}, u32[]{:S(2)}) %copy-start) | copy-done | bytes 524312
  2.3 0.0 copy-start.1
  2.3 1.0 %copy-done.1 = bf16[256,1024]{1,0:T(8,128)(2,1)S(1)} copy-done((bf16[256,1024]{1,0:T(8,128)(2,1)S(1)}, bf16[256,1024]{1,0:T(8,128)(2,1)}, u32[]{:S(2)}) %copy-start.1) | copy-done | bytes 524312
  3.4 0.0 copy-start.2
  3.4 1.0 %copy-done.2 = bf16[256,1024]{1,0:T(8,128)(2,1)S(1)} copy-done((bf16[256,1024]{1,0:T(8,128)(2,1)S(1)}, bf16[256,1024]{1,0:T(8,128)(2,1)}, u32[]{:S(2)}) %copy-start.2) | copy-done | bytes 524312
  4.4 0.0 copy-start.3
  4.4 1.0 %copy-done.3 = bf16[256,1024]{1,0:T(8,128)(2,1)S(1)} copy-done((bf16[256,1024]{1,0:T(8,128)(2,1)S(1)}, bf16[256,1024]{1,0:T(8,128)(2,1)}, u32[]{:S(2)}) %copy-start.3) | copy-done | bytes 524312
  5.5 0.0 copy-start.4
  5.5 1.0 %copy-done.4 = bf16[256,1024]{1,0:T(8,128)(2,1)S(1)} copy-done((bf16[256,1024]{1,0:T(8,128)(2,1)S(1)}, bf16[256,1024]{1,0:T(8,128)(2,1)}, u32[]{:S(2)}) %copy-start.4) | copy-done | bytes 524312
  6.5 0.0 copy-start.5
  6.5 0.7 %copy-done.5 = f32[8,256]{1,0:T(8,128)S(1)} copy-done((f32[8,256]{1,0:T(8,128)S(1)}, f32[8,256]{1,0:T(8,128)}, u32[]{:S(2)}) %copy-start.5) | copy-done | bytes 8216
  7.2 0.0 copy-start.6
  7.2 0.7 %copy-done.6 = f32[1024]{0:T(1024)S(1)} copy-done((f32[1024]{0:T(1024)S(1)}, f32[1024]{0:T(1024)}, u32[]{:S(2)}) %copy-start.6) | copy-done | bytes 4120
  7.9 55.6 %attention_both_ways.1 = (bf16[256,1024]{1,0:T(8,128)(2,1)S(1)}, bf16[256,1024]{1,0:T(8,128)(2,1)S(1)}, bf16[256,1024]{1,0:T(8,128)(2,1)S(1)}, bf16[256,1024]{1,0:T(8,128)(2,1)S(1)}) custom-call(bf16[256,1024]{1,0:T(8,128)(2,1)S(1)} %copy-done, bf16[256,1024]{1,0:T(8,128)(2,1)S(1)} %copy-done.1, bf16[256,1024]{1,0:T(8,128)(2,1)S(1)} %copy-done.2, ...), custom_call_target="tpu_custom_call" | custom-call | tf_op jit(solution)/shard_map/attention_both_ways/pallas_call | solution.py:319
  63.5 0.8 %copy.16 = bf16[256,1024]{1,0:T(8,128)(2,1)} copy(bf16[256,1024]{1,0:T(8,128)(2,1)S(1)} %get-tuple-element.8) | data formatting | bytes 1048576
  64.3 0.8 %copy.17 = bf16[256,1024]{1,0:T(8,128)(2,1)} copy(bf16[256,1024]{1,0:T(8,128)(2,1)S(1)} %get-tuple-element.9) | data formatting | bytes 1048576
  65.1 0.8 %copy.18 = bf16[256,1024]{1,0:T(8,128)(2,1)} copy(bf16[256,1024]{1,0:T(8,128)(2,1)S(1)} %get-tuple-element.10) | data formatting | bytes 1048576
  65.9 0.8 %copy.19 = bf16[256,1024]{1,0:T(8,128)(2,1)} copy(bf16[256,1024]{1,0:T(8,128)(2,1)S(1)} %get-tuple-element.11) | data formatting | bytes 1048576
Async XLA Ops:
  0.6 0.7 copy-start.7
  1.3 1.0 %copy-start = (bf16[256,1024]{1,0:T(8,128)(2,1)S(1)}, bf16[256,1024]{1,0:T(8,128)(2,1)}, u32[]{:S(2)}) copy-start(bf16[256,1024]{1,0:T(8,128)(2,1)} %q_ref.1) | copy-start | bytes 1572868
  2.3 1.0 %copy-start.1 = (bf16[256,1024]{1,0:T(8,128)(2,1)S(1)}, bf16[256,1024]{1,0:T(8,128)(2,1)}, u32[]{:S(2)}) copy-start(bf16[256,1024]{1,0:T(8,128)(2,1)} %k_ref.1) | copy-start | bytes 1572868
  3.4 1.0 %copy-start.2 = (bf16[256,1024]{1,0:T(8,128)(2,1)S(1)}, bf16[256,1024]{1,0:T(8,128)(2,1)}, u32[]{:S(2)}) copy-start(bf16[256,1024]{1,0:T(8,128)(2,1)} %v_ref.1) | copy-start | bytes 1572868
  4.4 1.0 %copy-start.3 = (bf16[256,1024]{1,0:T(8,128)(2,1)S(1)}, bf16[256,1024]{1,0:T(8,128)(2,1)}, u32[]{:S(2)}) copy-start(bf16[256,1024]{1,0:T(8,128)(2,1)} %gate_ref.1) | copy-start | bytes 1572868
  5.5 1.0 %copy-start.4 = (bf16[256,1024]{1,0:T(8,128)(2,1)S(1)}, bf16[256,1024]{1,0:T(8,128)(2,1)}, u32[]{:S(2)}) copy-start(bf16[256,1024]{1,0:T(8,128)(2,1)} %gout_ref.1) | copy-start | bytes 1572868
  6.5 0.7 %copy-start.5 = (f32[8,256]{1,0:T(8,128)S(1)}, f32[8,256]{1,0:T(8,128)}, u32[]{:S(2)}) copy-start(f32[8,256]{1,0:T(8,128)} %decay_ref.1) | copy-start | bytes 24580
  7.2 0.7 %copy-start.6 = (f32[1024]{0:T(1024)S(1)}, f32[1024]{0:T(1024)}, u32[]{:S(2)}) copy-start(f32[1024]{0:T(1024)} %param.14) | copy-start | bytes 12292

commit v2 on v1

--- a/solution.py
+++ b/solution.py
@@ -9,6 +9,7 @@
 
 HEAD_DIM = 128
 EPSILON = 1e-06
+VMEM_BYTES = 60 * 1024 * 1024
 MESH = pl.DeviceIdType.MESH
 F32 = jnp.float32
 BF16 = jnp.bfloat16
@@ -24,6 +25,23 @@
 def kernel(
     n_seq,
     n_head,
+    parts,
+    q_hbm,
+    k_hbm,
+    v_hbm,
+    decay_hbm,
+    starts_hbm,
+    gate_hbm,
+    gain_hbm,
+    gout_hbm,
+    dq_hbm,
+    dk_hbm,
+    dv_hbm,
+    dgate_hbm,
+    dq_ref,
+    dk_ref,
+    dv_ref,
+    dgate_ref,
     q_ref,
     k_ref,
     v_ref,
@@ -32,11 +50,8 @@
     gate_ref,
     gain_ref,
     gout_ref,
-    dq_ref,
-    dk_ref,
-    dv_ref,
-    dgate_ref,
     mine_ref,
+    cross_ref,
     theirs_ref,
     onward_ref,
     inbound_ref,
@@ -52,6 +67,9 @@
     dv_part_ref,
     bias_ref,
     sums_ref,
+    load_sem,
+    whole_sem,
+    column_sem,
     state_send,
     state_recv,
     chain_send,
@@ -71,6 +89,22 @@
     first = side == 0
     partner = seq + 1 - 2 * side
 
+    loads = {}
+    for place, (name, src, dst) in enumerate(
+        (
+            ("decay", decay_hbm, decay_ref),
+            ("starts", starts_hbm, starts_ref),
+            ("k", k_hbm, k_ref),
+            ("v", v_hbm, v_ref),
+            ("q", q_hbm, q_ref),
+            ("gain", gain_hbm, gain_ref),
+            ("gate", gate_hbm, gate_ref),
+            ("gout", gout_hbm, gout_ref),
+        )
+    ):
+        loads[name] = pltpu.make_async_copy(src, dst, load_sem.at[place])
+        loads[name].start()
+
     def cols(h):
         return slice(h * HEAD_DIM, (h + 1) * HEAD_DIM)
 
@@ -90,32 +124,6 @@
     @pl.when(link < links - 1)
     def _():
         greet(seq + 2, head)
-
-    row_ids = lax.broadcasted_iota(jnp.int32, (tokens, tokens), 0)
-    col_ids = lax.broadcasted_iota(jnp.int32, (tokens, tokens), 1)
-    causal = row_ids >= col_ids
-    lower = causal.astype(F32)
-    decay = decay_ref[...]
-    sum_row = mm(decay, lower, 1, 1, HIGHEST)
-    sum_col = mm(lower, decay, 1, 1, HIGHEST)
-    ids_col = lax.broadcasted_iota(jnp.int32, (tokens, 1), 0)
-    ids_row = lax.broadcasted_iota(jnp.int32, (1, tokens), 1)
-    count_col = jnp.zeros((tokens, 1), jnp.int32)
-    count_row = jnp.zeros((1, tokens), jnp.int32)
-    latest = jnp.int32(0)
-    for j in range(starts_ref.shape[1]):
-        start = starts_ref[0, j]
-        count_col += (ids_col >= start).astype(jnp.int32)
-        count_row += (ids_row >= start).astype(jnp.int32)
-        latest += (start < tokens).astype(jnp.int32)
-    inward = jnp.where(count_col == 0, jnp.exp(sum_col), 0.0)
-    outward = jnp.where(
-        count_col == latest, jnp.exp(sum_col[tokens - 1 : tokens, :] - sum_col), 0.0
-    )
-    through = jnp.where(latest == 0, jnp.exp(sum_row[:, tokens - 1 : tokens]), 0.0)
-    through_ref[0] = jnp.broadcast_to(through, (heads, HEAD_DIM))
-    keep = jnp.logical_and(causal, count_col == count_row)
-    bias_ref[...] = jnp.where(keep, 0.0, -1e30)
 
     def remote(src, dst, send, recv, s, h):
         return pltpu.make_async_remote_copy(
@@ -131,9 +139,16 @@
         through_ref.at[0], through_ref.at[1], through_sem.at[0], through_sem.at[1], partner, head
     )
 
+    early = heads // 2
+    part_rows = HEAD_DIM // parts
+
+    def rows(p):
+        return slice(p * part_rows, (p + 1) * part_rows)
+
     def exchange(way, h):
+        source = mine_ref if h < early else cross_ref
         return remote(
-            mine_ref.at[way, h],
+            source.at[way, h],
             theirs_ref.at[way, h],
             state_send.at[way, h],
             state_recv.at[way, h],
@@ -141,14 +156,13 @@
             head,
         )
 
-    def chain(way, h):
-        target = seq + 2 if way == 0 else seq - 2
+    def chain(way, h, p):
         return remote(
-            onward_ref.at[way, h],
-            inbound_ref.at[way, h],
-            chain_send.at[way, h],
-            chain_recv.at[way, h],
-            target,
+            onward_ref.at[way, h, pl.ds(p * part_rows, part_rows)],
+            inbound_ref.at[way, h, pl.ds(p * part_rows, part_rows)],
+            chain_send.at[way, h * parts + p],
+            chain_recv.at[way, h * parts + p],
+            seq + 2 if way == 0 else seq - 2,
             head,
         )
 
@@ -158,27 +172,110 @@
     def has_previous(way):
         return link > 0 if way == 0 else link < links - 1
 
-    def pass_on(way, h):
-        leads = first if way == 0 else jnp.logical_not(first)
+    def leads(way):
+        return first if way == 0 else jnp.logical_not(first)
+
+    def throughs(h):
+        return through_ref[0, h : h + 1, :], through_ref[1, h : h + 1, :]
+
+    def pair_then_chain(way, h):
         exchange(way, h).wait_recv()
-        mine = mine_ref[way, h]
-        theirs = theirs_ref[way, h]
-        t_mine = through_ref[0, h : h + 1, :]
-        t_theirs = through_ref[1, h : h + 1, :]
-        pair = jnp.where(leads, t_theirs, 1.0) * mine + jnp.where(leads, 1.0, t_mine) * theirs
-
-        @pl.when(has_previous(way))
-        def _():
-            chain(way, h).wait_recv()
-
-        arrived = inbound_ref[way, h]
-
-        @pl.when(has_next(way))
-        def _():
-            onward_ref[way, h] = t_mine * t_theirs * arrived + pair
-            chain(way, h).start()
-
-        return jnp.where(leads, 1.0, t_theirs) * arrived + jnp.where(leads, 0.0, 1.0) * theirs
+        t_mine, t_theirs = throughs(h)
+        state = []
+        for p in range(parts):
+            theirs = theirs_ref[way, h, rows(p)]
+            pair = (
+                jnp.where(leads(way), t_theirs, 1.0) * mine_ref[way, h, rows(p)]
+                + jnp.where(leads(way), 1.0, t_mine) * theirs
+            )
+
+            @pl.when(has_previous(way))
+            def _():
+                chain(way, h, p).wait_recv()
+
+            arrived = inbound_ref[way, h, rows(p)]
+
+            @pl.when(has_next(way))
+            def _():
+                onward_ref[way, h, rows(p)] = t_mine * t_theirs * arrived + pair
+                chain(way, h, p).start()
+
+            state.append(
+                jnp.where(leads(way), 1.0, t_theirs) * arrived
+                + jnp.where(leads(way), 0.0, 1.0) * theirs
+            )
+        return jnp.concatenate(state, axis=0)
+
+    def chain_alone(way, h):
+        t_mine, t_theirs = throughs(h)
+        for p in range(parts):
+            mine = mine_ref[way, h, rows(p)]
+
+            @pl.when(has_previous(way))
+            def _():
+                chain(way, h, p).wait_recv()
+
+            arrived = inbound_ref[way, h, rows(p)]
+
+            @pl.when(has_next(way))
+            def _():
+                onward_ref[way, h, rows(p)] = (
+                    t_mine * t_theirs * arrived + jnp.where(leads(way), t_theirs, 1.0) * mine
+                )
+                chain(way, h, p).start()
+
+            cross_ref[way, h, rows(p)] = (
+                jnp.where(leads(way), t_mine, 1.0) * arrived
+                + jnp.where(leads(way), 1.0, 0.0) * mine
+            )
+        exchange(way, h).start()
+
+    def pair_last(way, h):
+        exchange(way, h).wait_recv()
+        _, t_theirs = throughs(h)
+        return jnp.where(leads(way), 1.0, t_theirs) * inbound_ref[way, h] + theirs_ref[way, h]
+
+    def scan(way, local_state, work, use):
+        pairs = [h for i in range(early) for h in (i, early + i)] + list(range(2 * early, heads))
+        for h in pairs:
+            mine_ref[way, h] = local_state(h)
+            if h < early:
+                exchange(way, h).start()
+            else:
+                if way == 0 and h == early:
+                    through_copy.wait_recv()
+
+                @pl.when(jnp.logical_not(has_previous(way)))
+                def _():
+                    chain_alone(way, h)
+
+        later = list(range(heads))
+        later = later[early:] + later[:early]
+        ready = 0
+        for ready in range(2):
+            work(later[ready])
+        ready = 2
+        for h in range(early, heads):
+
+            @pl.when(has_previous(way))
+            def _():
+                chain_alone(way, h)
+
+            if ready < heads:
+                work(later[ready])
+                ready += 1
+        for h in pairs:
+            if h < early:
+                state = pair_then_chain(way, h)
+            else:
+                state = pair_last(way, h)
+            while ready <= later.index(h):
+                work(later[ready])
+                ready += 1
+            use(h, state.astype(BF16))
+            if ready < heads:
+                work(later[ready])
+                ready += 1
 
     for way in range(2):
 
@@ -186,15 +283,45 @@
         def _():
             inbound_ref[way] = jnp.zeros(inbound_ref.shape[1:], F32)
 
+    row_ids = lax.broadcasted_iota(jnp.int32, (tokens, tokens), 0)
+    col_ids = lax.broadcasted_iota(jnp.int32, (tokens, tokens), 1)
+    causal = row_ids >= col_ids
+    lower = causal.astype(F32)
+    loads["decay"].wait()
+    loads["starts"].wait()
+    decay = decay_ref[...]
+    latest = jnp.int32(0)
+    for j in range(starts_ref.shape[1]):
+        latest += (starts_ref[0, j] < tokens).astype(jnp.int32)
+    through = jnp.where(latest == 0, jnp.exp(jnp.sum(decay, axis=1, keepdims=True)), 0.0)
+    through_ref[0] = jnp.broadcast_to(through, (heads, HEAD_DIM))
     pl.semaphore_wait(
         barrier,
         n_head + (link > 0).astype(jnp.int32) + (link < links - 1).astype(jnp.int32),
     )
     through_copy.start()
-    for h in range(heads):
+    sum_col = mm(lower, decay, 1, 1, HIGHEST)
+    sum_row = mm(decay, lower, 1, 1, HIGHEST)
+    ids_col = lax.broadcasted_iota(jnp.int32, (tokens, 1), 0)
+    ids_row = lax.broadcasted_iota(jnp.int32, (1, tokens), 1)
+    count_col = jnp.zeros((tokens, 1), jnp.int32)
+    count_row = jnp.zeros((1, tokens), jnp.int32)
+    for j in range(starts_ref.shape[1]):
+        start = starts_ref[0, j]
+        count_col += (ids_col >= start).astype(jnp.int32)
+        count_row += (ids_row >= start).astype(jnp.int32)
+    outward = jnp.where(
+        count_col == latest, jnp.exp(sum_col[tokens - 1 : tokens, :] - sum_col), 0.0
+    )
+    inward = jnp.where(count_col == 0, jnp.exp(sum_col), 0.0)
+    keep = jnp.logical_and(causal, count_col == count_row)
+    bias_ref[...] = jnp.where(keep, 0.0, -1e30)
+    loads["k"].wait()
+    loads["v"].wait()
+
+    def forward_state(h):
         scaled = (k_ref[:, cols(h)].astype(F32) * outward[:, h : h + 1]).astype(BF16)
-        mine_ref[0, h] = mm(scaled, v_ref[:, cols(h)], 0, 0)
-        exchange(0, h).start()
+        return mm(scaled, v_ref[:, cols(h)], 0, 0)
 
     def within(h):
         q = q_ref[:, cols(h)]
@@ -209,23 +336,28 @@
         dnormed_ref[:, cols(h)] = dnormed
         dgate_part_ref[:, cols(h)] = dnormed * (1.0 - opening)
 
-    squares = jnp.zeros((tokens, HEAD_DIM), F32)
-    products = jnp.zeros((tokens, HEAD_DIM), F32)
-    ahead = 2
-    for h in range(min(ahead, heads)):
-        within(h)
-    through_copy.wait_recv()
-    for h in range(heads):
-        state = pass_on(0, h).astype(BF16)
+    sums = [jnp.zeros((tokens, HEAD_DIM), F32)] * 2
+
+    def attend(h, state):
         enter_ref[h] = state
         attended = attended_ref[:, cols(h)] + inward[:, h : h + 1] * mm(
             q_ref[:, cols(h)], state, 1, 0
         )
         attended_ref[:, cols(h)] = attended
-        squares += attended * attended
-        products += dnormed_ref[:, cols(h)] * attended
-        if h + ahead < heads:
-            within(h + ahead)
+        sums[0] += attended * attended
+        sums[1] += dnormed_ref[:, cols(h)] * attended
+
+    waited = []
+
+    def first_work(h):
+        if not waited:
+            for name in ("q", "gain", "gate", "gout"):
+                loads[name].wait()
+            waited.append(True)
+        within(h)
+
+    scan(0, forward_state, first_work, attend)
+    squares, products = sums
 
     ones = jnp.ones((8, HEAD_DIM), F32)
     square_rows = mm(ones, squares, 1, 1, HIGHEST)
@@ -261,12 +393,15 @@
     inverse = scalars[:, 0:1]
     pull = scalars[:, 1:2]
 
-    grads = []
-    for h in range(heads):
+    grads = {}
+
+    def backward_state(h):
         grad = (dnormed_ref[:, cols(h)] * inverse - attended_ref[:, cols(h)] * pull).astype(BF16)
-        grads.append(grad)
-        mine_ref[1, h] = mm(qscaled_ref[:, cols(h)], grad, 0, 0)
-        exchange(1, h).start()
+        grads[h] = grad
+        return mm(qscaled_ref[:, cols(h)], grad, 0, 0)
+
+    stores = []
+    worked = []
 
     def inside(h):
         q = q_ref[:, cols(h)]
@@ -281,19 +416,30 @@
         dgate_ref[:, cols(h)] = (
             dgate_part_ref[:, cols(h)] * attended_ref[:, cols(h)] * inverse
         ).astype(BF16)
-
-    for h in range(min(ahead, heads)):
-        inside(h)
-    for h in range(heads):
-        state = pass_on(1, h).astype(BF16)
+        worked.append(h)
+        if len(worked) == heads:
+            for place, (src, dst) in enumerate(((dq_ref, dq_hbm), (dgate_ref, dgate_hbm))):
+                copy = pltpu.make_async_copy(src, dst, whole_sem.at[place])
+                copy.start()
+                stores.append(copy)
+
+    def finish(h, state):
         scale = outward[:, h : h + 1]
         dk = dk_part_ref[:, cols(h)] + scale * mm(v_ref[:, cols(h)], state, 1, 1)
         dv = dv_part_ref[:, cols(h)] + scale * mm(k_ref[:, cols(h)], state, 1, 0)
         dk_ref[:, cols(h)] = dk.astype(BF16)
         dv_ref[:, cols(h)] = dv.astype(BF16)
-        if h + ahead < heads:
-            inside(h + ahead)
-
+        for place, (src, dst) in enumerate(((dk_ref, dk_hbm), (dv_ref, dv_hbm))):
+            copy = pltpu.make_async_copy(
+                src.at[:, cols(h)], dst.at[:, cols(h)], column_sem.at[place, h]
+            )
+            copy.start()
+            stores.append(copy)
+
+    scan(1, backward_state, inside, finish)
+
+    for copy in stores:
+        copy.wait()
     through_copy.wait_send()
     for copy in sum_copies:
         copy.wait_send()
@@ -304,7 +450,17 @@
         @pl.when(has_next(way))
         def _():
             for h in range(heads):
-                chain(way, h).wait_send()
+                for p in range(parts):
+                    chain(way, h, p).wait_send()
+
+
+def store(*refs):
+    sem = refs[-1]
+    copies = [pltpu.make_async_copy(refs[i], refs[4 + i], sem.at[i]) for i in range(4)]
+    for copy in copies:
+        copy.start()
+    for copy in copies:
+        copy.wait()
 
 
 def local(queries, key_vectors, values, decay_log, doc_starts, gate_logits, norm_gain, grad_out):
@@ -312,16 +468,29 @@
     n_head = lax.axis_size("head")
     tokens, width = queries.shape
     heads = width // HEAD_DIM
-    vmem = pl.BlockSpec(memory_space=pltpu.VMEM)
-    smem = pl.BlockSpec(memory_space=pltpu.SMEM)
+    hbm = pl.BlockSpec(memory_space=pltpu.HBM)
+    parts = 2
     states = (2, heads, HEAD_DIM, HEAD_DIM)
     out = jax.ShapeDtypeStruct((tokens, width), BF16)
-    return pl.pallas_call(
-        functools.partial(kernel, n_seq, n_head),
+    results = pl.pallas_call(
+        functools.partial(kernel, n_seq, n_head, parts),
         out_shape=(out, out, out, out),
-        in_specs=[vmem, vmem, vmem, vmem, smem, vmem, vmem, vmem],
-        out_specs=(vmem, vmem, vmem, vmem),
+        in_specs=[hbm] * 8,
+        out_specs=(hbm, hbm, hbm, hbm),
         scratch_shapes=[
+            pltpu.VMEM((tokens, width), BF16),
+            pltpu.VMEM((tokens, width), BF16),
+            pltpu.VMEM((tokens, width), BF16),
+            pltpu.VMEM((tokens, width), BF16),
+            pltpu.VMEM((tokens, width), BF16),
+            pltpu.VMEM((tokens, width), BF16),
+            pltpu.VMEM((tokens, width), BF16),
+            pltpu.VMEM(decay_log.shape, F32),
+            pltpu.SMEM(doc_starts.shape, jnp.int32),
+            pltpu.VMEM((tokens, width), BF16),
+            pltpu.VMEM((1, width), F32),
+            pltpu.VMEM((tokens, width), BF16),
+            pltpu.VMEM(states, F32),
             pltpu.VMEM(states, F32),
             pltpu.VMEM(states, F32),
             pltpu.VMEM(states, F32),
@@ -338,16 +507,19 @@
             pltpu.VMEM((tokens, width), F32),
             pltpu.VMEM((tokens, tokens), F32),
             pltpu.VMEM((n_head, 8, tokens), F32),
+            pltpu.SemaphoreType.DMA((8,)),
+            pltpu.SemaphoreType.DMA((2,)),
             pltpu.SemaphoreType.DMA((2, heads)),
             pltpu.SemaphoreType.DMA((2, heads)),
             pltpu.SemaphoreType.DMA((2, heads)),
-            pltpu.SemaphoreType.DMA((2, heads)),
+            pltpu.SemaphoreType.DMA((2, heads * parts)),
+            pltpu.SemaphoreType.DMA((2, heads * parts)),
             pltpu.SemaphoreType.DMA((2,)),
             pltpu.SemaphoreType.DMA((max(n_head - 1, 1),)),
             pltpu.SemaphoreType.DMA((max(n_head - 1, 1),)),
         ],
         compiler_params=pltpu.CompilerParams(
-            collective_id=0, has_side_effects=True, vmem_limit_bytes=48 * 1024 * 1024
+            collective_id=0, has_side_effects=True, vmem_limit_bytes=VMEM_BYTES
         ),
         name="attention_both_ways",
     )(
@@ -360,6 +532,15 @@
         norm_gain.reshape(1, width),
         grad_out,
     )
+    return pl.pallas_call(
+        store,
+        out_shape=(out, out, out, out),
+        in_specs=[hbm] * 4,
+        out_specs=(hbm, hbm, hbm, hbm),
+        scratch_shapes=[pltpu.SemaphoreType.DMA((4,))],
+        compiler_params=pltpu.CompilerParams(vmem_limit_bytes=VMEM_BYTES),
+        name="store_results",
+    )(*results)
 
 
 def solution(mesh):

time: 67.1 us -> 119 us (1.77)
  Pallas kernels: 55.6 us -> 118 us
  local copies, waits for them, and re-layouts: 10.4 us -> 0 us
    pallas_call x1 -> x2, Pallas kernels: 55.6 us -> 118 us  [the longest x1 64.7 us: local(): pl.pallas_call(store, out_shape=(out, out, out, out), in_specs=[hbm] * 4,...]
    unnamed x20 -> x0, local copies, waits for them, and re-layouts: 10.4 us -> none
where the time goes in v2:
time: 119 us
  Pallas kernels  118 us (99%)
    pallas_call x1, Pallas kernels, local(): pl.pallas_call(store, out_shape=(out, out, out, out), in_specs=[hbm] * 4,...  64.7 us
    pallas_call x1, Pallas kernels, local(): pl.pallas_call(functools.partial(kernel, n_seq, n_head, parts), out_shape...  53.6 us

profile of v2, /device:TPU:0, one launch (start us, length us, event | category | flops | bytes accessed | tf_op | source)
XLA Modules:
  0.0 118.9 jit_solution(7628116842544732974)
XLA Ops:
  0.6 53.6 %attention_both_ways.1 = (bf16[256,1024]{1,0:T(8,128)(2,1)}, bf16[256,1024]{1,0:T(8,128)(2,1)}, bf16[256,1024]{1,0:T(8,128)(2,1)}, bf16[256,1024]{1,0:T(8,128)(2,1)}) custom-call(bf16[256,1024]{1,0:T(8,128)(2,1)} %q_hbm.1, bf16[256,1024]{1,0:T(8,128)(2,1)} %k_hbm.1, bf16[256,1024]{1,0:T(8,128)(2,1)} %v_hbm.1, f32[8,256]{1,0:T(8,128)} %decay_hbm.1, ...), custom_call_target="tpu_custom_call" | custom-call | tf_op jit(solution)/shard_map/attention_both_ways/pallas_call | solution.py:475
  54.3 64.7 %store_results.1 = (bf16[256,1024]{1,0:T(8,128)(2,1)}, bf16[256,1024]{1,0:T(8,128)(2,1)}, bf16[256,1024]{1,0:T(8,128)(2,1)}, bf16[256,1024]{1,0:T(8,128)(2,1)}) custom-call(bf16[256,1024]{1,0:T(8,128)(2,1)} %get-tuple-element.8.refs_0_, bf16[256,1024]{1,0:T(8,128)(2,1)} %get-tuple-element.9.refs_1_, bf16[256,1024]{1,0:T(8,128)(2,1)} %get-tuple-element.10.refs_2_, ...), custom_call_target="tpu_custom_call" | custom-call | tf_op jit(solution)/shard_map/store_results/pallas_call | solution.py:535

commit v3 on v2

--- a/solution.py
+++ b/solution.py
@@ -455,11 +455,15 @@
 
 
 def store(*refs):
-    sem = refs[-1]
-    copies = [pltpu.make_async_copy(refs[i], refs[4 + i], sem.at[i]) for i in range(4)]
-    for copy in copies:
-        copy.start()
-    for copy in copies:
+    held, sem = refs[8:12], refs[12]
+    loads = [pltpu.make_async_copy(refs[i], held[i], sem.at[i]) for i in range(4)]
+    stores = [pltpu.make_async_copy(held[i], refs[4 + i], sem.at[4 + i]) for i in range(4)]
+    for load in loads:
+        load.start()
+    for i in range(4):
+        loads[i].wait()
+        stores[i].start()
+    for copy in stores:
         copy.wait()
 
 
@@ -537,7 +541,7 @@
         out_shape=(out, out, out, out),
         in_specs=[hbm] * 4,
         out_specs=(hbm, hbm, hbm, hbm),
-        scratch_shapes=[pltpu.SemaphoreType.DMA((4,))],
+        scratch_shapes=[pltpu.VMEM((tokens, width), BF16)] * 4 + [pltpu.SemaphoreType.DMA((8,))],
         compiler_params=pltpu.CompilerParams(vmem_limit_bytes=VMEM_BYTES),
         name="store_results",
     )(*results)

time: 119 us -> 56.9 us (0.48)
  Pallas kernels: 118 us -> 56 us
    pallas_call x1, Pallas kernels: 64.7 us -> 2.42 us  [local(): pl.pallas_call(store, out_shape=(out, out, out, out), in_specs=[hbm] * 4,...]
where the time goes in v3:
time: 56.9 us; the launch traced here: 56.7 us
  Pallas kernels  56 us (98%)
  between operations  0.64 us (1%)
    pallas_call x1, Pallas kernels, local(): pl.pallas_call(functools.partial(kernel, n_seq, n_head, parts), out_shape...  53.6 us
    pallas_call x1, Pallas kernels, local(): pl.pallas_call(store, out_shape=(out, out, out, out), in_specs=[hbm] * 4,...  2.42 us

profile of v3, /device:TPU:0, one launch (start us, length us, event | category | flops | bytes accessed | tf_op | source)
XLA Modules:
  0.0 56.7 jit_solution(12971597491917226774)
XLA Ops:
  0.6 53.6 %attention_both_ways.1 = (bf16[256,1024]{1,0:T(8,128)(2,1)}, bf16[256,1024]{1,0:T(8,128)(2,1)}, bf16[256,1024]{1,0:T(8,128)(2,1)}, bf16[256,1024]{1,0:T(8,128)(2,1)}) custom-call(bf16[256,1024]{1,0:T(8,128)(2,1)} %q_hbm.1, bf16[256,1024]{1,0:T(8,128)(2,1)} %k_hbm.1, bf16[256,1024]{1,0:T(8,128)(2,1)} %v_hbm.1, f32[8,256]{1,0:T(8,128)} %decay_hbm.1, ...), custom_call_target="tpu_custom_call" | custom-call | tf_op jit(solution)/shard_map/attention_both_ways/pallas_call | solution.py:479
  54.3 2.4 %store_results.1 = (bf16[256,1024]{1,0:T(8,128)(2,1)}, bf16[256,1024]{1,0:T(8,128)(2,1)}, bf16[256,1024]{1,0:T(8,128)(2,1)}, bf16[256,1024]{1,0:T(8,128)(2,1)}) custom-call(bf16[256,1024]{1,0:T(8,128)(2,1)} %get-tuple-element.8.refs_0_, bf16[256,1024]{1,0:T(8,128)(2,1)} %get-tuple-element.9.refs_1_, bf16[256,1024]{1,0:T(8,128)(2,1)} %get-tuple-element.10.refs_2_, ...), custom_call_target="tpu_custom_call" | custom-call | tf_op jit(solution)/shard_map/store_results/pallas_call | solution.py:539

commit v4 on v3

--- a/solution.py
+++ b/solution.py
@@ -473,7 +473,7 @@
     tokens, width = queries.shape
     heads = width // HEAD_DIM
     hbm = pl.BlockSpec(memory_space=pltpu.HBM)
-    parts = 2
+    parts = 1
     states = (2, heads, HEAD_DIM, HEAD_DIM)
     out = jax.ShapeDtypeStruct((tokens, width), BF16)
     results = pl.pallas_call(

time: 56.9 us -> 58 us (1.019)
  Pallas kernels: 56 us -> 57.2 us
    pallas_call x1, Pallas kernels: 53.6 us -> 54.8 us  [local(): pl.pallas_call(functools.partial(kernel, n_seq, n_head, parts), out_shape...]
where the time goes in v4:
time: 58 us; the launch traced here: 57.8 us
  Pallas kernels  57.2 us (99%)
  between operations  0.64 us (1%)
    pallas_call x1, Pallas kernels, local(): pl.pallas_call(functools.partial(kernel, n_seq, n_head, parts), out_shape...  54.8 us
    pallas_call x1, Pallas kernels, local(): pl.pallas_call(store, out_shape=(out, out, out, out), in_specs=[hbm] * 4,...  2.42 us

profile of v4, /device:TPU:0, one launch (start us, length us, event | category | flops | bytes accessed | tf_op | source)
XLA Modules:
  0.0 57.8 jit_solution(5047490004719543649)
XLA Ops:
  0.6 54.8 %attention_both_ways.1 = (bf16[256,1024]{1,0:T(8,128)(2,1)}, bf16[256,1024]{1,0:T(8,128)(2,1)}, bf16[256,1024]{1,0:T(8,128)(2,1)}, bf16[256,1024]{1,0:T(8,128)(2,1)}) custom-call(bf16[256,1024]{1,0:T(8,128)(2,1)} %q_hbm.1, bf16[256,1024]{1,0:T(8,128)(2,1)} %k_hbm.1, bf16[256,1024]{1,0:T(8,128)(2,1)} %v_hbm.1, f32[8,256]{1,0:T(8,128)} %decay_hbm.1, ...), custom_call_target="tpu_custom_call" | custom-call | tf_op jit(solution)/shard_map/attention_both_ways/pallas_call | solution.py:479
  55.4 2.4 %store_results.1 = (bf16[256,1024]{1,0:T(8,128)(2,1)}, bf16[256,1024]{1,0:T(8,128)(2,1)}, bf16[256,1024]{1,0:T(8,128)(2,1)}, bf16[256,1024]{1,0:T(8,128)(2,1)}) custom-call(bf16[256,1024]{1,0:T(8,128)(2,1)} %get-tuple-element.8.refs_0_, bf16[256,1024]{1,0:T(8,128)(2,1)} %get-tuple-element.9.refs_1_, bf16[256,1024]{1,0:T(8,128)(2,1)} %get-tuple-element.10.refs_2_, ...), custom_call_target="tpu_custom_call" | custom-call | tf_op jit(solution)/shard_map/store_results/pallas_call | solution.py:539
